TPU v7x, 256 devices: a whole 4x4x8 slice. The times are simulated.
256 devices in a mesh: dp: 64 (over y, z, core), bal: 4 (over x).
Axes of the slice: x: 4, y: 4, z: 8, core: 2. Of those that a mesh axis runs over, the one named last changes fastest.
Arguments:
- queries: bfloat16 [3, 512, 128, 1664], P(None, ('dp', 'bal')), may hold values from -30 to 30
- keys: bfloat16 [3, 512, 128, 1664], P(None, ('dp', 'bal')), may hold values from -6 to 6
- values: bfloat16 [3, 512, 128, 1664], P(None, ('dp', 'bal')), may hold values from -15 to 15
- cotangent: bfloat16 [3, 512, 128, 1664], P(None, ('dp', 'bal')), may hold values from -6 to 6
- counts: int32 [3, 64, 4], P(None, 'dp'), may hold values from 0 to 2, as said below
- out_weight: bfloat16 [1664, 1664], P('dp'), may hold values from -0.15625 to 0.15625
Outputs:
- attended: bfloat16 [3, 512, 128, 1664], P(None, ('dp', 'bal'))
- weight_grad: float32 [1664, 1664], P('dp')
Inputs may be any that keep to these rules, and one draw needn't show every extreme that they name: In every micro-batch the 4 counts of one group sum to exactly 4, and one of them equals 2.
All inputs are finite; a program needn't handle non-finite values.
Results may differ from a plain program's by a relative error of at most 0.0058.
Values may be sent and summed in bfloat16 or wider, within the bound.
A program may use at most 128 MiB of HBM per device.

v0:
```python
import math

import jax
import jax.numpy as jnp
from jax import lax
from jax.sharding import PartitionSpec as P

HEADS = 13
HD = 128
TT = 128
MICRO = 3
BSLOT = 1


def attend_tiles(queries, keys, values):
    tile_count, tile_len, head_width = queries.shape
    shaped = (tile_count, tile_len, HEADS, HD)
    scores = jnp.einsum(
        "nqhc,nkhc->nhqk",
        queries.reshape(shaped),
        keys.reshape(shaped),
        preferred_element_type=jnp.float32,
    ) * HD ** (-0.5)
    scores = scores - jnp.max(scores, axis=-1, keepdims=True)
    expons = jnp.exp(scores)
    normed = (expons / jnp.sum(expons, axis=-1, keepdims=True)).astype(jnp.bfloat16)
    context = jnp.einsum(
        "nhqk,nkhc->nqhc", normed, values.reshape(shaped), preferred_element_type=jnp.float32
    )
    return context.reshape(tile_count, tile_len, head_width).astype(jnp.bfloat16)


def project(context_rows, out_weight):
    return jnp.dot(
        context_rows,
        lax.all_gather(out_weight, "dp", axis=0, tiled=True),
        preferred_element_type=jnp.float32,
    )


def gradient_rows(context_rows, cot_rows):
    whole = lax.dot_general(
        context_rows, cot_rows, (((0,), (0,)), ((), ())), preferred_element_type=jnp.float32
    )
    quarter = lax.psum_scatter(whole, "bal", scatter_dimension=1, tiled=True)
    block = lax.psum_scatter(quarter, "dp", scatter_dimension=0, tiled=True)
    return lax.all_gather(block, "bal", axis=1, tiled=True)


def local(queries, keys, values, cotangent, counts, out_weight):
    micro, own, tile_len, head_width = queries.shape
    features = cotangent.shape[-1]
    member = lax.axis_index("bal")
    mine = counts[:, 0, :]
    my_count = lax.dynamic_index_in_dim(mine, member, 1, keepdims=False)
    live = jnp.arange(own)[None, :] < my_count[:, None]
    flat = (micro * own, tile_len, head_width)
    context = attend_tiles(queries.reshape(flat), keys.reshape(flat), values.reshape(flat))
    context = jnp.where(live.reshape(micro * own, 1, 1), context, jnp.zeros_like(context))
    context_rows = context.reshape(micro * own * tile_len, head_width)
    cot_rows = cotangent.reshape(micro * own * tile_len, features)
    projected = project(context_rows, out_weight)
    attended = projected.astype(jnp.bfloat16).reshape(micro, own, tile_len, features)
    summed = gradient_rows(context_rows, cot_rows)
    live_tokens = MICRO * BSLOT * TT * lax.axis_size("dp") * lax.axis_size("bal")
    return (attended, summed / math.sqrt(live_tokens))


def solution(mesh):
    return jax.shard_map(
        local,
        mesh=mesh,
        in_specs=(
            P(None, ("dp", "bal"), None, None),
            P(None, ("dp", "bal"), None, None),
            P(None, ("dp", "bal"), None, None),
            P(None, ("dp", "bal"), None, None),
            P(None, "dp", None),
            P("dp", None),
        ),
        out_specs=(P(None, ("dp", "bal"), None, None), P("dp", None)),
        check_vma=False,
    )
```

profile of v0, /device:TPU:1, one launch (start us, length us, event | category | flops | bytes accessed | tf_op | source)
XLA Modules:
  0.0 362.9 jit_solution(11940168663126297677)
XLA Ops:
  8.0 0.0 copy-start
  8.0 0.0 reduce-scatter.3.cloned.1.call-start
  8.1 1.1 dynamic-slice_reduce_fusion
  9.1 0.1 iota_compare_fusion
  9.2 0.1 lt.31
  9.3 4.5 %copy.33 = bf16[3,2,128,1664]{2,3,1,0:T(8,128)(2,1)} copy(bf16[3,2,128,1664]{3,2,1,0:T(8,128)(2,1)} %param.6) | data formatting | bytes 5111808 | tf_op args[0]
  13.8 4.5 %copy.34 = bf16[3,2,128,1664]{2,3,1,0:T(8,128)(2,1)} copy(bf16[3,2,128,1664]{3,2,1,0:T(8,128)(2,1)} %param.7) | data formatting | bytes 5111808 | tf_op args[1]
  18.3 4.4 %copy.37 = bf16[3,2,128,1664]{2,3,1,0:T(8,128)(2,1)} copy(bf16[3,2,128,1664]{3,2,1,0:T(8,128)(2,1)} %param.8) | data formatting | bytes 5111808 | tf_op args[2]
  22.7 6.7 %fusion.18 = (f32[6,13,128]{2,1,0:T(8,128)S(1)}, f32[6,13,128,128]{2,3,1,0:T(8,128)}) fusion(bf16[6,128,13,128]{1,3,2,0:T(8,128)(2,1)} %bitcast.39, bf16[6,128,13,128]{1,3,2,0:T(8,128)(2,1)} %bitcast.40), kind=kOutput, calls=%fused_computation.26 | convolution fusion | flops 330989696 | bytes 10263552 | tf_op jit(solution)/shard_map/sub | solution.py:24
  29.4 5.2 %fusion.12 = bf16[6,13,128,128]{3,2,1,0:T(8,128)(2,1)S(1)} fusion(bf16[6,128,13,128]{1,3,2,0:T(8,128)(2,1)} %bitcast.44, f32[6,13,128,128]{2,3,1,0:T(8,128)} %get-tuple-element.3, f32[6,13,128]{2,1,0:T(8,128)S(1)} %get-tuple-element.2), kind=kOutput, calls=%fused_computation.16 | convolution fusion | flops 330989568 | bytes 10263552 | tf_op jit(solution)/shard_map/nhqk,nkhc->nqhc/dot_general | solution.py:27
  34.6 0.0 copy-start.2
  34.6 0.2 select_bitcast_fusion
  34.9 1.2 copy-done.2
  36.1 1.7 copy.41
  37.8 0.0 copy-done
  37.8 7.9 %fusion.5 = f32[1664,1664]{0,1:T(8,128)} fusion(bf16[768,1664]{1,0:T(8,128)(2,1)S(1)} %bitcast.38, bf16[96,8,13,128]{3,2,1,0:T(8,128)(2,1)S(1)} %bitcast.43), kind=kOutput, calls=%fused_computation.7 | convolution fusion | flops 4253024256 | bytes 16187392 | tf_op jit(solution)/shard_map/dot_general | solution.py:42
  45.7 0.0 reduce-scatter.3.cloned.1.call-update
  45.8 0.0 copy-start.3
  45.8 0.0 all-gather.4.cloned.1.call-start
  45.8 0.5 all-gather.4.cloned.1.call-update
  46.3 0.2 all-reduce.3.cloned.1.call-start
  46.6 108.0 %reduce-scatter.3.cloned.1.call-done = f32[1664,416]{0,1:T(8,128)} async-done(((f32[1664,1664]{0,1:T(8,128)}), f32[1664,416]{0,1:T(8,128)}) %reduce-scatter.3.cloned.1.call-update) | async-done | bytes 2768912 | tf_op jit(solution)/shard_map/reduce_scatter | solution.py:45
  154.6 0.0 all-reduce.3.cloned.1.call-update
  154.6 0.0 copy-done.3
  154.6 0.0 copy-start.4
  154.6 3.4 copy.40
  158.0 0.0 copy-done.4
  158.0 0.6 dynamic-slice.1
  159.3 0.1 broadcast_bitcast_fusion
  159.3 0.0 all-gather.4.cloned.1.call-done
  159.3 8.3 %reshape.43 = bf16[1664,1664]{1,0:T(8,128)(2,1)} reshape(bf16[64,26,1664]{2,1,0:T(8,128)(2,1)} %all-gather.4.cloned.1.call-done) | data formatting | bytes 11075584
  167.6 0.0 copy-start.1
  167.6 10.8 %convolution_convert_fusion = bf16[768,1664]{1,0:T(8,128)(2,1)} fusion(bf16[1664,1664]{1,0:T(8,128)(2,1)} %reshape.43, bf16[96,8,13,128]{3,2,1,0:T(8,128)(2,1)} %bitcast.42, pred[768]{0:T(1024)(128)(4,1)S(1)} %broadcast_bitcast_fusion), kind=kOutput, calls=%fused_computation.5 | convolution fusion | flops 4255580160 | bytes 10650368 | tf_op jit(solution)/shard_map/dot_general | solution.py:34
  178.4 165.1 %all-reduce.3.cloned.1.call-done = f32[1664,416]{0,1:T(8,128)} async-done(((f32[1664,416]{0,1:T(8,128)}), f32[1664,416]{0,1:T(8,128)}) %all-reduce.3.cloned.1.call-update) | async-done | bytes 2768912
  343.4 1.1 dynamic-slice_bitcast_fusion
  344.6 0.1 copy.42
  344.7 9.7 %all-gather.1 = f32[4,416,26]{1,2,0:T(8,128)S(1)} all-gather(f32[1,416,26]{1,2,0:T(8,128)S(1)} %copy.42), channel_id=1, replica_groups=mesh['dp'=64,'bal'=4] {'bal'}, dimensions={0}, use_global_device_ids=true | all-gather | bytes 216320 | tf_op jit(solution)/shard_map/all_gather | solution.py:47
  354.4 0.1 copy.43
  354.5 0.9 reshape.47
  355.4 0.0 copy-done.1
  (1 shorter events, 0.0 us)
Async XLA Ops:
  8.0 29.8 %copy-start = (bf16[3,2,128,1664]{3,2,1,0:T(8,128)(2,1)S(1)}, bf16[3,2,128,1664]{3,2,1,0:T(8,128)(2,1)}, u32[]{:S(2)}) copy-start(bf16[3,2,128,1664]{3,2,1,0:T(8,128)(2,1)} %param.9) | copy-start | bytes 7667716
  8.0 146.6 %reduce-scatter.3.cloned.1.call-start = ((), (), s32[]{:S(2)}) async-start(), calls=%async_computation.1 | async-start | bytes 13844480 | tf_op jit(solution)/shard_map/reduce_scatter | solution.py:45
  34.6 1.5 copy-start.2
  45.8 108.9 %copy-start.3 = (bf16[6,13,128,128]{3,2,1,0:T(8,128)(2,1)S(1)}, bf16[6,13,128,128]{3,2,1,0:T(8,128)(2,1)}, u32[]{:S(2)}) copy-start(bf16[6,13,128,128]{3,2,1,0:T(8,128)(2,1)} %copy-done.2) | copy-start | bytes 7667716
  45.8 113.6 %all-gather.4.cloned.1.call-start = ((), (), s32[]{:S(2)}) async-start(), calls=%async_computation.2 | async-start | bytes 6922240 | tf_op jit(solution)/shard_map/all_gather | solution.py:36
  46.3 297.1 %all-reduce.3.cloned.1.call-start = ((), (), s32[]{:S(2)}) async-start(), calls=%async_computation.3 | async-start | bytes 5537792
  154.6 3.4 copy-start.4
  167.6 187.8 %copy-start.1 = (bf16[3,2,128,1664]{3,2,1,0:T(8,128)(2,1)S(1)}, bf16[3,2,128,1664]{3,2,1,0:T(8,128)(2,1)}, u32[]{:S(2)}) copy-start(bf16[3,2,128,1664]{3,2,1,0:T(8,128)(2,1)} %param.9) | copy-start | bytes 7667716
Sparse Core Ops, SparseCore 0:
  45.9 108.6 reduce-scatter.2
Sparse Core Ops, SparseCore 1:
  49.0 86.1 all-gather.3
  154.7 188.7 all-reduce.2
where the time goes:
time: 368 us; the launch traced here: 363 us
  waiting for transfers between devices  274 us (74%)
  local copies, waits for them, and re-layouts  32.1 us (9%)
  matrix products  30.6 us (8%)
  between operations  16.2 us (4%)
  blocking collectives  9.67 us (3%)
    unnamed x4, waiting for transfers between devices  166 us
    reduce_scatter x1, waiting for transfers between devices, gradient_rows(): quarter = lax.psum_scatter(whole, 'bal', scatter_dimension=1, tiled=True)  108 us
    unnamed x17, local copies, waits for them, and re-layouts  24.7 us
    dot_general x1, matrix products, project(): jnp.dot(context_rows, lax.all_gather(out_weight, 'dp', axis=0, tiled=True...  10.8 us
    all_gather x1, blocking collectives, gradient_rows(): return lax.all_gather(block, 'bal', axis=1, tiled=True)  9.67 us
    dot_general x1, matrix products, gradient_rows(): lax.dot_general(context_rows, cot_rows, (((0,), (0,)), ((), ())), preferr...  7.89 us
  transfers between devices with their start and end apart: 3, of which 2 were waited for; matrix products, arithmetic and copies ran while one was open for 6% of the time, Pallas kernels for 0%

commit v1 on v0

v1 whole, which is shorter than its diff:
```python
import math

import jax
import jax.numpy as jnp
from jax import lax
from jax.experimental import pallas as pl
from jax.experimental.pallas import tpu as pltpu
from jax.sharding import PartitionSpec as P

HEADS = 13
HD = 128
TT = 128
MICRO = 3
OWN = 2
F = 1664
ROWS = MICRO * OWN * TT
NX, NY, NZ = 4, 4, 8
HALF = 208
BLK = 26
PAD = 32
WA = 768
WB = 896
SCALE = 1.0 / math.sqrt(98304.0)
MESH = pl.DeviceIdType.MESH
F32 = jnp.float32
BF = jnp.bfloat16
NSEM = 136


def kernel(q_hbm, k_hbm, v_hbm, cot_hbm, counts, w_ref, out_hbm, grad_ref,
           q, k, v, cot, ctx, ctxt, att, wa, wb, wra, wrb,
           gs, gown, gr, gs3, gown3, gr3,
           xs2, xs1, xs3, xt0, xt1, rl1, rl2, rl3, rr1, rr2, rr3,
           ys, yr, zs, zo, zr, fr,
           in_sem, out_sem, ssem, rsem):
    dp = lax.axis_index("dp")
    x = lax.axis_index("bal")
    c = lax.rem(dp, 2)
    z = lax.rem(lax.div(dp, 2), NZ)
    y = lax.div(dp, 2 * NZ)
    sib = 1 - c
    zl = lax.rem(z, 4)
    owner = lax.div(z, 4) == c

    def dev(yy, zz, cc, xx):
        return {"dp": (yy * NZ + zz) * 2 + cc, "bal": xx}

    def at_x(d):
        return lax.rem(x + d, NX)

    def at_y(d):
        return lax.rem(y + d, NY)

    def at_z(d):
        return lax.rem(z + d, NZ)

    right_x, left_x = dev(y, z, c, at_x(1)), dev(y, z, c, at_x(3))
    up_y, down_y = dev(at_y(1), z, c, x), dev(at_y(3), z, c, x)
    up_z, down_z = dev(y, at_z(1), c, x), dev(y, at_z(7), c, x)
    sibling = dev(y, z, sib, x)

    used = [0]
    unsent = []

    def copy(src, dst, to):
        i = used[0]
        used[0] += 1
        one = pltpu.make_async_remote_copy(
            src_ref=src, dst_ref=dst, send_sem=ssem.at[i], recv_sem=rsem.at[i],
            device_id=to, device_id_type=MESH)
        one.start()
        unsent.append(one)
        return one

    loads = {}
    n_in = 0
    for m in range(MICRO):
        for name, src, dst in (("q", q_hbm, q), ("k", k_hbm, k), ("v", v_hbm, v)):
            one = pltpu.make_async_copy(src.at[pl.ds(2 * m, 2)], dst.at[pl.ds(2 * m, 2)], in_sem.at[n_in])
            one.start()
            loads[name, m] = one
            n_in += 1
    load_cot = pltpu.make_async_copy(cot_hbm, cot, in_sem.at[n_in])
    load_cot.start()

    wa[c, y, z, pl.ds(16, 16), :] = jnp.zeros((16, WA), BF)
    wb[c, y, z, pl.ds(16, 16), :] = jnp.zeros((16, WB), BF)
    wa[c, y, z, pl.ds(0, BLK), :] = w_ref[:, 0:WA]
    wb[c, y, z, pl.ds(0, BLK), :] = w_ref[:, WA:F]

    barrier = pltpu.get_barrier_semaphore()
    partners = [sibling]
    partners += [dev(y, z, cc, at_x(d)) for d in (1, 2, 3) for cc in (c, sib)]
    partners += [dev(at_y(d), z, c, x) for d in (1, 2, 3)]
    partners += [dev(y, at_z(d), c, x) for d in range(1, NZ)]
    for one in partners:
        pl.semaphore_signal(barrier, inc=1, device_id=one, device_id_type=MESH)
    pl.semaphore_wait(barrier, len(partners))

    w_sib = []

    def a_line(zz):
        return wa.at[c, :, zz]

    def a_half(zz, start):
        return wa.at[c, :, zz, pl.ds(start, 16), :]

    def b_block(zz):
        return wb.at[c, y, zz]

    def b_half(zz, start):
        return wb.at[c, y, zz, pl.ds(start, 16), :]

    def to_sib(ref):
        w_sib.append(copy(ref, ref, sibling))

    state = {}

    def a_start():
        mine = wa.at[c, y, z]
        state["ay"] = [copy(mine, mine, dev(at_y(d), z, c, x)) for d in (1, 2, 3)]

    def ring_step(key, step, whole, half):
        if step < 4:
            right = whole(at_z(8 - (step - 1)))
            left = whole(at_z(step - 1))
        else:
            right = half(at_z(5), 0)
            left = half(at_z(3), 16)
        state[key] = [copy(right, right, up_z), copy(left, left, down_z)]

    def ring_wait(key):
        for one in state[key]:
            one.wait_recv()

    def a_ring(step):
        ring_wait("ay" if step == 1 else "az")
        ring_step("az", step, a_line, a_half)
        if step == 1:
            to_sib(a_line(z))
        else:
            to_sib(a_line(at_z(8 - (step - 1))))
            to_sib(a_line(at_z(step - 1)))

    def a_end():
        ring_wait("az")
        to_sib(a_line(at_z(4)))

    def b_ring(step):
        if step > 1:
            ring_wait("bz")
        ring_step("bz", step, b_block, b_half)

    def b_y1():
        ring_wait("bz")
        line = wb.at[c, y]
        state["by"] = [copy(line, line, up_y), copy(line, line, down_y)]
        to_sib(line)

    def b_y2():
        ring_wait("by")
        below, above = at_y(3), at_y(1)
        lo = wb.at[c, below, pl.ds(0, 4)]
        hi = wb.at[c, above, pl.ds(4, 4)]
        state["by"] = [copy(lo, lo, up_y), copy(hi, hi, down_y)]
        to_sib(wb.at[c, below])
        to_sib(wb.at[c, above])

    def b_end():
        ring_wait("by")
        to_sib(wb.at[c, at_y(2)])

    def attend(m):
        for name in ("q", "k", "v"):
            loads[name, m].wait()

        def tile(j, carry):
            t = 2 * m + j
            alive = j < counts[m, 0, x]
            row = pl.multiple_of(t * TT, TT)
            for h in range(HEADS):
                cols = slice(h * HD, (h + 1) * HD)
                s = lax.dot_general(q[t, :, cols], k[t, :, cols], (((1,), (1,)), ((), ())),
                                    preferred_element_type=F32) * (HD ** -0.5)
                e = jnp.exp(s - jnp.max(s, axis=-1, keepdims=True))
                p = (e / jnp.sum(e, axis=-1, keepdims=True)).astype(BF)
                o = jnp.dot(p, v[t, :, cols], preferred_element_type=F32)
                o = jnp.where(alive, o, jnp.zeros_like(o))
                ctx[pl.ds(row, TT), cols] = o.astype(BF)
                ctxt[cols, pl.ds(row, TT)] = o.T.astype(BF)
            return carry

        lax.fori_loop(0, OWN, tile, 0)

    def grad_piece(half, col, width, store):
        def body(yy, carry):
            row = pl.multiple_of(yy * (2 * HALF) + half * HALF, 16)
            r = jnp.dot(ctxt[pl.ds(row, HALF), :], cot[:, col:col + width], preferred_element_type=F32)
            store(yy, r)
            return carry

        lax.fori_loop(0, NY, body, 0)

    def grad_sib(u):
        if u < 3:
            def store(yy, r):
                for t in range(4):
                    gs[u, t, yy] = r[:, t * 128:(t + 1) * 128].astype(BF)
            grad_piece(sib, u * 512, 512, store)
            state["g", u] = copy(gs.at[u], gr.at[u], sibling)
        else:
            def store(yy, r):
                gs3[yy] = r.astype(BF)
            grad_piece(sib, 1536, 128, store)
            state["g", u] = copy(gs3, gr3, sibling)

    def grad_own(u):
        if u < 3:
            def store(yy, r):
                for t in range(4):
                    gown[u, t, yy] = r[:, t * 128:(t + 1) * 128]
            grad_piece(c, u * 512, 512, store)
        else:
            def store(yy, r):
                gown3[yy] = r
            grad_piece(c, 1536, 128, store)

    def two(body):
        lax.fori_loop(0, 2, lambda i, carry: (body(i), carry)[1], 0)

    def x1(u):
        state["g", u].wait_recv()
        o2, o1, o3 = at_x(2), at_x(1), at_x(3)

        def pair(t, yy):
            return (gown[u, t, yy] + gr[u, t, yy].astype(F32)).astype(BF)

        def body(i):
            xs2[u, i] = pair(o2, i)
            xs2[u, i + 2] = pair(o2, i + 2)
            xs1[u, i] = pair(o1, i + 2)
            xs3[u, i] = pair(o3, i)

        two(body)
        state["x", u] = [
            copy(xs2.at[u, pl.ds(0, 2)], rl1.at[u], right_x),
            copy(xs2.at[u, pl.ds(2, 2)], rr1.at[u], left_x),
            copy(xs1.at[u], rl2.at[u], right_x),
            copy(xs3.at[u], rr2.at[u], left_x),
        ]

    def x2(u):
        state["x", u][0].wait_recv()
        state["x", u][1].wait_recv()
        o1, o3 = at_x(1), at_x(3)

        def body(i):
            xt0[u, i] = (gown[u, o1, i] + gr[u, o1, i].astype(F32) + rl1[u, i].astype(F32)).astype(BF)
            xt1[u, i] = (gown[u, o3, i + 2] + gr[u, o3, i + 2].astype(F32) + rr1[u, i].astype(F32)).astype(BF)

        two(body)
        state["x", u] += [
            copy(xt0.at[u], rl3.at[u], right_x),
            copy(xt1.at[u], rr3.at[u], left_x),
        ]

    def x3(u):
        if u < 3:
            for i in (2, 3, 4, 5):
                state["x", u][i].wait_recv()

            def body(i):
                a = (gown[u, x, i] + gr[u, x, i].astype(F32)
                     + rl3[u, i].astype(F32) + rr2[u, i].astype(F32))
                b = (gown[u, x, i + 2] + gr[u, x, i + 2].astype(F32)
                     + rl2[u, i].astype(F32) + rr3[u, i].astype(F32))
                gown[u, x, i] = a
                gown[u, x, i + 2] = b
                ys[u, i] = a.astype(BF)
                ys[u, i + 2] = b.astype(BF)
        else:
            state["g", u].wait_recv()

            def body(i):
                for j in (i, i + 2):
                    a = gown3[j] + gr3[j].astype(F32)
                    gown3[j] = a
                    ys[u, j] = a.astype(BF)

        two(body)
        state["y", u] = [
            copy(ys.at[u, at_y(d)], yr.at[u, d - 1], dev(at_y(d), z, c, x)) for d in (1, 2, 3)]

    def y2(u):
        for one in state["y", u]:
            one.wait_recv()
        total = gown[u, x, y] if u < 3 else gown3[y]
        for d in range(3):
            total = total + yr[u, d].astype(F32)
        zo[u] = total
        zs[u] = total.astype(BF)
        base = used[0]
        used[0] += 7
        copies = []
        for i in range(4):
            zt = 4 * c + i
            slot = lax.rem(z - zt + NZ, NZ) - 1
            slot = jnp.maximum(slot, 0)
            one = pltpu.make_async_remote_copy(
                src_ref=zs.at[u, pl.ds(48 * i, 64)], dst_ref=zr.at[u, slot],
                send_sem=ssem.at[base + i], recv_sem=rsem.at[base + slot],
                device_id=dev(y, zt, c, x), device_id_type=MESH)

            @pl.when(zt != z)
            def _():
                one.start()

            copies.append((zt, one))
        state["z", u] = (base, copies)

    def z2(u):
        base, copies = state["z", u]
        fbase = used[0]
        used[0] += 8

        @pl.when(owner)
        def _():
            total = zo[u, pl.ds(pl.multiple_of(48 * zl, 16), 64), :]
            for d in range(7):
                pltpu.make_async_remote_copy(
                    src_ref=zs.at[u, pl.ds(0, 64)], dst_ref=zr.at[u, d],
                    send_sem=ssem.at[base], recv_sem=rsem.at[base + d],
                    device_id=up_z, device_id_type=MESH).wait_recv()
                total = total + zr[u, d].astype(F32)
            fr[u, x] = total.astype(BF)
            n = 0
            for d in range(4):
                for cc in (c, sib):
                    if d == 0 and cc is c:
                        continue
                    pltpu.make_async_remote_copy(
                        src_ref=fr.at[u, x], dst_ref=fr.at[u, x],
                        send_sem=ssem.at[fbase + n], recv_sem=rsem.at[fbase + d],
                        device_id=dev(y, z, cc, at_x(d)), device_id_type=MESH).start()
                    n += 1

        state["f", u] = fbase

    def f2(u):
        fbase = state["f", u]

        def arrived(d):
            src = fr.at[u, at_x(4 - d)]
            pltpu.make_async_remote_copy(
                src_ref=src, dst_ref=src, send_sem=ssem.at[fbase], recv_sem=rsem.at[fbase + d],
                device_id=sibling, device_id_type=MESH).wait_recv()

        @pl.when(jnp.logical_not(owner))
        def _():
            arrived(0)

        for d in (1, 2, 3):
            arrived(d)
        if u < 3:
            for t in range(4):
                col = (4 * u + t) * 128
                grad_ref[:, col:col + 128] = fr[u, t].astype(F32) * SCALE
        else:
            total = fr[u, 0].astype(F32)
            for t in (1, 2, 3):
                total = total + fr[u, t].astype(F32)
            grad_ref[:, 1536:F] = total * SCALE

    def drain():
        for one in unsent:
            one.wait_send()
        for u in range(4):
            base, copies = state["z", u]
            for zt, one in copies:
                @pl.when(zt != z)
                def _():
                    one.wait_send()
            fbase = state["f", u]

            @pl.when(owner)
            def _():
                for n in range(7):
                    pltpu.make_async_remote_copy(
                        src_ref=fr.at[u, x], dst_ref=fr.at[u, x], send_sem=ssem.at[fbase + n],
                        recv_sem=rsem.at[fbase], device_id=sibling, device_id_type=MESH).wait_send()

    def place(src, dst, width):
        r = lax.broadcasted_iota(jnp.int32, (HALF, 8 * PAD), 0)
        s = lax.broadcasted_iota(jnp.int32, (HALF, 8 * PAD), 1)
        cc, zz, j = s // (4 * PAD), (s // PAD) % 4, s % PAD
        pick = jnp.where((j < BLK) & (r == (zz * 2 + cc) * BLK + j), 1.0, 0.0).astype(BF)

        def body(g, carry):
            yy, z0 = g // 2, (g % 2) * 4
            a = src[0, yy, pl.ds(z0, 4)].reshape(4 * PAD, width)
            b = src[1, yy, pl.ds(z0, 4)].reshape(4 * PAD, width)
            r = jnp.dot(pick, jnp.concatenate([a, b], axis=0), preferred_element_type=F32)
            dst[pl.ds(pl.multiple_of(g * HALF, 16), HALF), :] = r.astype(BF)
            return carry

        lax.fori_loop(0, 8, body, 0)

    def project(w, col, width, lo, hi):
        def body(t, carry):
            rows = pl.ds(pl.multiple_of(t * 256, 256), 256)
            r = jnp.dot(ctx[rows, :], w[...], preferred_element_type=F32)
            att[rows, col:col + width] = r.astype(BF)
            return carry

        lax.fori_loop(lo, hi, body, 0)

    out_copies = []

    def store_out(i):
        rows = pl.ds(256 * i, 256)
        one = pltpu.make_async_copy(att.at[rows], out_hbm.at[rows], out_sem.at[i])
        one.start()
        out_copies.append(one)

    a_start()
    b_ring(1)
    attend(0)
    a_ring(1)
    b_ring(2)
    attend(1)
    b_ring(3)
    attend(2)
    a_ring(2)
    b_ring(4)
    load_cot.wait()
    grad_sib(0)
    grad_own(0)
    x1(0)
    grad_sib(1)
    b_y1()
    grad_own(1)
    x1(1)
    a_ring(3)
    x2(0)
    grad_sib(2)
    grad_own(2)
    x1(2)
    grad_sib(3)
    grad_own(3)
    b_y2()
    x2(1)
    x3(0)
    a_ring(4)
    x3(3)
    x2(2)
    y2(0)
    y2(3)
    x3(1)
    b_end()
    a_end()
    z2(0)
    z2(3)
    y2(1)
    for one in w_sib:
        one.wait_recv()
    place(wa, wra, WA)
    place(wb, wrb, WB)
    x3(2)
    z2(1)
    project(wra, 0, WA, 0, 3)
    y2(2)
    project(wrb, WA, WB, 0, 1)
    store_out(0)
    z2(2)
    project(wrb, WA, WB, 1, 3)
    store_out(1)
    store_out(2)
    for u in (0, 3, 1, 2):
        f2(u)
    drain()
    for one in out_copies:
        one.wait()
    assert used[0] <= NSEM, used[0]


def core(queries, keys, values, cotangent, counts, weight):
    any_spec = pl.BlockSpec(memory_space=pl.ANY)
    vmem = pl.BlockSpec(memory_space=pltpu.VMEM)
    tiles = (MICRO * OWN, TT, F)
    V = pltpu.VMEM
    scratch = [
        V(tiles, BF), V(tiles, BF), V(tiles, BF), V((ROWS, F), BF),
        V((ROWS, F), BF), V((F, ROWS), BF), V((ROWS, F), BF),
        V((2, NY, NZ, PAD, WA), BF), V((2, NY, NZ, PAD, WB), BF), V((F, WA), BF), V((F, WB), BF),
        V((3, 4, NY, HALF, 128), BF), V((3, 4, NY, HALF, 128), F32), V((3, 4, NY, HALF, 128), BF),
        V((NY, HALF, 128), BF), V((NY, HALF, 128), F32), V((NY, HALF, 128), BF),
        V((3, 4, HALF, 128), BF),
    ]
    scratch += [V((3, 2, HALF, 128), BF)] * 10
    scratch += [
        V((4, NY, HALF, 128), BF), V((4, 3, HALF, 128), BF),
        V((4, HALF, 128), BF), V((4, HALF, 128), F32), V((4, 7, 64, 128), BF), V((4, 4, 64, 128), BF),
        pltpu.SemaphoreType.DMA((10,)), pltpu.SemaphoreType.DMA((3,)),
        pltpu.SemaphoreType.DMA((NSEM,)), pltpu.SemaphoreType.DMA((NSEM,)),
    ]
    return pl.pallas_call(
        kernel,
        out_shape=[jax.ShapeDtypeStruct((ROWS, F), BF), jax.ShapeDtypeStruct((64, F), F32)],
        in_specs=[any_spec] * 4 + [pl.BlockSpec(memory_space=pltpu.SMEM), vmem],
        out_specs=[any_spec, vmem],
        scratch_shapes=scratch,
        compiler_params=pltpu.CompilerParams(
            collective_id=0, has_side_effects=True, vmem_limit_bytes=60 * 1024 * 1024),
        cost_estimate=pl.CostEstimate(flops=9_200_000_000, bytes_accessed=20_000_000, transcendentals=1_300_000),
    )(queries, keys, values, cotangent, counts, weight)


def local(queries, keys, values, cotangent, counts, out_weight):
    tiles = (MICRO * OWN, TT, F)
    attended, rows = core(
        queries.reshape(tiles), keys.reshape(tiles), values.reshape(tiles),
        cotangent.reshape(ROWS, F), counts, out_weight)
    dp = lax.axis_index("dp")
    c, z = dp % 2, (dp // 2) % NZ
    grad = lax.dynamic_slice_in_dim(rows, 4 * (z % 4) + BLK * c, BLK, 0)
    return (attended.reshape(MICRO, OWN, TT, F), grad)


def solution(mesh):
    return jax.shard_map(
        local,
        mesh=mesh,
        in_specs=(
            P(None, ("dp", "bal"), None, None),
            P(None, ("dp", "bal"), None, None),
            P(None, ("dp", "bal"), None, None),
            P(None, ("dp", "bal"), None, None),
            P(None, "dp", None),
            P("dp", None),
        ),
        out_specs=(P(None, ("dp", "bal"), None, None), P("dp", None)),
        check_vma=False,
    )
```

time: 368 us -> 99 us (0.27); the launches traced: 363 us -> 98.8 us
  waiting for transfers between devices: 274 us -> 0 us
  Pallas kernels: 0 us -> 93 us
  matrix products: 30.6 us -> 0 us
  local copies, waits for them, and re-layouts: 32.1 us -> 5.05 us
  between operations: 16.2 us -> 0.7 us
  blocking collectives: 9.67 us -> 0 us
    unnamed x4 -> x0, waiting for transfers between devices: 166 us -> none
    reduce_scatter x1 -> x0, waiting for transfers between devices: 108 us -> none  [gradient_rows(): quarter = lax.psum_scatter(whole, 'bal', scatter_dimension=1, tiled=True)]
    pallas_call x0 -> x1, Pallas kernels: none -> 93 us  [core(): pl.pallas_call(kernel, out_shape=[jax.ShapeDtypeStruct((ROWS, F), BF), ja...]
    dot_general x3 -> x0, matrix products: 23.8 us -> none  [the longest x1 10.8 us: project(): jnp.dot(context_rows, lax.all_gather(out_weight, 'dp', axis=0, tiled=True...]
    unnamed x17 -> x1, local copies, waits for them, and re-layouts: 24.7 us -> 3.38 us
    all_gather x1 -> x0, blocking collectives: 9.67 us -> none  [gradient_rows(): return lax.all_gather(block, 'bal', axis=1, tiled=True)]
    sub x1 -> x0, matrix products: 6.74 us -> none  [attend_tiles(): scores = scores - jnp.max(scores, axis=-1, keepdims=True)]
  transfers between devices with their start and end apart: 3 -> 0, of which waited for: 2 -> 0; matrix products, arithmetic and copies ran while one was open for 6% -> 0% of each run, Pallas kernels for 0% -> 0%
where the time goes in v1:
time: 99 us; the launch traced here: 98.8 us
  Pallas kernels  93 us (94%)
  local copies, waits for them, and re-layouts  5.05 us (5%)
    pallas_call x1, Pallas kernels, core(): pl.pallas_call(kernel, out_shape=[jax.ShapeDtypeStruct((ROWS, F), BF), ja...  93 us
    unnamed x1, local copies, waits for them, and re-layouts  3.38 us

profile of v1, /device:TPU:1, one launch (start us, length us, event | category | flops | bytes accessed | tf_op | source)
XLA Modules:
  0.0 98.8 jit_solution(3522037820136537204)
XLA Ops:
  0.7 93.0 %shard_map.77 = (bf16[768,1664]{1,0:T(8,128)(2,1)}, f32[64,1664]{1,0:T(8,128)}) custom-call(bf16[6,128,1664]{2,1,0:T(8,128)(2,1)} %bitcast.6, bf16[6,128,1664]{2,1,0:T(8,128)(2,1)} %bitcast.7, bf16[6,128,1664]{2,1,0:T(8,128)(2,1)} %bitcast.8, bf16[768,1664]{1,0:T(8,128)(2,1)} %bitcast.9, s32[3,1,4]{2,1,0:T(1,128)} %counts.1, bf16[26,1664]{1,0:T(8,128)(2,1)} %w_ref.1), custom_call_target="tpu_custom_call" | custom-call | flops 9200000000 | bytes 20000000 | tf_op jit(solution)/shard_map/pallas_call | solution.py:506
  93.7 1.7 %constant_dynamic-slice_fusion = f32[26,1664]{1,0:T(8,128)} fusion(f32[64,1664]{1,0:T(8,128)} %get-tuple-element.5, s32[]{:T(128)S(6)} %select_n.26), kind=kLoop, calls=%fused_computation | loop fusion | bytes 346116 | tf_op jit(solution)/shard_map/dynamic_slice | solution.py:525
  95.4 3.4 %copy.9 = bf16[3,2,128,1664]{3,2,1,0:T(8,128)(2,1)} copy(bf16[3,2,128,1664]{3,2,1,0:T(8,128)(2,1)} %bitcast.5) | data formatting | bytes 5111808

commit v2 on v1

v2 whole, which is shorter than its diff:
```python
import math

import jax
import jax.numpy as jnp
from jax import lax
from jax.experimental import pallas as pl
from jax.experimental.pallas import tpu as pltpu
from jax.sharding import PartitionSpec as P

HEADS = 13
HD = 128
TT = 128
MICRO = 3
OWN = 2
F = 1664
ROWS = MICRO * OWN * TT
NX, NY, NZ = 4, 4, 8
HALF = 208
BLK = 26
PAD = 32
WA = 768
WB = 896
SCALE = 1.0 / math.sqrt(98304.0)
EXP_SCALE = HD ** -0.5 * 1.4426950408889634
MESH = pl.DeviceIdType.MESH
F32 = jnp.float32
BF = jnp.bfloat16
NSEM = 48


def kernel(q_hbm, k_hbm, v_hbm, cot_hbm, counts, w_ref, out_hbm, grad_ref,
           q, k, v, cot, ctx, ctxt, att, wa, wb, wra, wrb,
           gs, gown, gr, gs3, gown3, gr3,
           xs2, xs1, xs3, xt, ra, rb,
           ys, yr, zs, zo, zr, fr,
           in_sem, out_sem, ssem, rsem):
    dp = lax.axis_index("dp")
    x = lax.axis_index("bal")
    c = lax.rem(dp, 2)
    z = lax.rem(lax.div(dp, 2), NZ)
    y = lax.div(dp, 2 * NZ)
    sib = 1 - c
    zl = lax.rem(z, 4)
    owner = lax.div(z, 4) == c

    def dev(yy, zz, cc, xx):
        return {"dp": (yy * NZ + zz) * 2 + cc, "bal": xx}

    def at_x(d):
        return lax.rem(x + d, NX)

    def at_y(d):
        return lax.rem(y + d, NY)

    def at_z(d):
        return lax.rem(z + d, NZ)

    right_x, left_x = dev(y, z, c, at_x(1)), dev(y, z, c, at_x(3))
    up_y, down_y = dev(at_y(1), z, c, x), dev(at_y(3), z, c, x)
    up_z, down_z = dev(y, at_z(1), c, x), dev(y, at_z(7), c, x)
    sibling = dev(y, z, sib, x)

    ids = {}

    def sem(group):
        return ids.setdefault(group, len(ids))

    def remote(group, src, dst, to):
        i = sem(group)
        return pltpu.make_async_remote_copy(
            src_ref=src, dst_ref=dst, send_sem=ssem.at[i], recv_sem=rsem.at[i],
            device_id=to, device_id_type=MESH)

    def send(group, src, dst, to):
        remote(group, src, dst, to).start()

    sizes = {}

    def arrived(group, size):
        sizes[group] = size
        remote(group, size, size, sibling).wait_recv()

    loads = {}
    n_in = 0
    for m in range(MICRO):
        for name, src, dst in (("q", q_hbm, q), ("k", k_hbm, k), ("v", v_hbm, v)):
            one = pltpu.make_async_copy(src.at[pl.ds(2 * m, 2)], dst.at[pl.ds(2 * m, 2)], in_sem.at[n_in])
            one.start()
            loads[name, m] = one
            n_in += 1
    load_cot = pltpu.make_async_copy(cot_hbm, cot, in_sem.at[n_in])
    load_cot.start()

    barrier_sem = pltpu.get_barrier_semaphore()
    partners = [sibling]
    partners += [dev(y, z, cc, at_x(d)) for d in (1, 2, 3) for cc in (c, sib)]
    partners += [dev(at_y(d), z, c, x) for d in (1, 2, 3)]
    partners += [dev(y, at_z(d), c, x) for d in range(1, NZ)]
    for one in partners:
        pl.semaphore_signal(barrier_sem, inc=1, device_id=one, device_id_type=MESH)

    wa[c, y, 4, pl.ds(16, 16), :] = jnp.zeros((16, WA), BF)
    wb[c, y, 4, pl.ds(16, 16), :] = jnp.zeros((16, WB), BF)
    wa[c, y, 4, pl.ds(0, BLK), :] = w_ref[:, 0:WA]
    wb[c, y, 4, pl.ds(0, BLK), :] = w_ref[:, WA:F]

    def barrier():
        pl.semaphore_wait(barrier_sem, len(partners))

    def line(r):
        return wa.at[c, :, r]

    def a0():
        mine = wa.at[c, y, 4]
        for d in (1, 2, 3):
            send("ay", mine, mine, dev(at_y(d), z, c, x))

    def a_ring(step):
        if step < 4:
            send(("az", step), line(5 - step), line(4 - step), up_z)
            send(("az", step), line(3 + step), line(4 + step), down_z)
        else:
            send(("az", step), wa.at[c, :, 1, pl.ds(0, 16), :], wa.at[c, :, 0, pl.ds(0, 16), :], up_z)
            send(("az", step), wa.at[c, :, 7, pl.ds(16, 16), :], wa.at[c, :, 0, pl.ds(16, 16), :], down_z)

    def a_sib(lo, n):
        ref = wa.at[c, :, pl.ds(lo, n)]
        send("as", ref, ref, sibling)

    def a1():
        arrived("ay", wa.at[c, pl.ds(0, 3), 4])
        a_ring(1)

    def a2():
        arrived(("az", 1), wa.at[c, :, pl.ds(0, 2)])
        a_ring(2)

    def a3():
        arrived(("az", 2), wa.at[c, :, pl.ds(0, 2)])
        a_ring(3)
        a_sib(2, 5)

    def a4():
        arrived(("az", 3), wa.at[c, :, pl.ds(0, 2)])
        a_ring(4)

    def a5():
        arrived(("az", 4), line(0))
        a_sib(0, 2)
        a_sib(7, 1)

    def block(r):
        return wb.at[c, y, r]

    def b_ring(step):
        if step < 4:
            send(("bz", step), block(5 - step), block(4 - step), up_z)
            send(("bz", step), block(3 + step), block(4 + step), down_z)
        else:
            send(("bz", step), wb.at[c, y, 1, pl.ds(0, 16), :], wb.at[c, y, 0, pl.ds(0, 16), :], up_z)
            send(("bz", step), wb.at[c, y, 7, pl.ds(16, 16), :], wb.at[c, y, 0, pl.ds(16, 16), :], down_z)

    def b_pass(group, yy, lo, n, to):
        ref = wb.at[c, yy, pl.ds(lo, n)]
        send(group, ref, ref, to)

    def b0():
        b_ring(1)
        for to in (up_y, down_y):
            b_pass("by0", y, 4, 1, to)

    def b1():
        arrived(("bz", 1), wb.at[c, 0, pl.ds(0, 2)])
        b_ring(2)

    def b2():
        arrived(("bz", 2), wb.at[c, 0, pl.ds(0, 2)])
        b_ring(3)
        for to in (up_y, down_y):
            b_pass("by1", y, 2, 2, to)
            b_pass("by1", y, 5, 2, to)

    def b3():
        arrived(("bz", 3), wb.at[c, 0, pl.ds(0, 2)])
        b_ring(4)

    def b4():
        arrived(("bz", 4), block(0))
        for to in (up_y, down_y):
            b_pass("by2", y, 0, 2, to)
            b_pass("by2", y, 7, 1, to)
        b_pass("bs", y, 0, 8, sibling)

    def b5():
        arrived("by0", wb.at[c, 0, pl.ds(0, 2)])
        arrived("by1", wb.at[c, 0])
        b_pass("bw1", at_y(3), 2, 2, up_y)
        b_pass("bw1", at_y(1), 4, 3, down_y)

    def b6():
        arrived("by2", wb.at[c, 0, pl.ds(0, 6)])
        b_pass("bw2", at_y(3), 0, 2, up_y)
        b_pass("bw2", at_y(1), 7, 1, down_y)
        b_pass("bs", at_y(3), 0, 8, sibling)
        b_pass("bs", at_y(1), 0, 8, sibling)

    def b7():
        arrived("bw1", wb.at[c, 0, pl.ds(0, 5)])
        arrived("bw2", wb.at[c, 0, pl.ds(0, 3)])
        b_pass("bs", at_y(2), 0, 8, sibling)

    def attend(m):
        for name in ("q", "k", "v"):
            loads[name, m].wait()

        def tile(j, carry):
            t = 2 * m + j
            alive = j < counts[m, 0, x]
            row = pl.multiple_of(t * TT, TT)
            heads = [slice(h * HD, (h + 1) * HD) for h in range(HEADS)]
            scores = [lax.dot_general(k[t, :, h], q[t, :, h], (((1,), (1,)), ((), ())),
                                      preferred_element_type=F32) for h in heads]
            turned = [v[t, :, h].T for h in heads]
            normed = []
            for s in scores:
                e = jnp.exp2((s - jnp.max(s, axis=0, keepdims=True)) * EXP_SCALE)
                normed.append((e * (1.0 / jnp.sum(e, axis=0, keepdims=True))).astype(BF))
            parts = [jnp.dot(vt, p, preferred_element_type=F32) for vt, p in zip(turned, normed)]
            for h, o in enumerate(parts):
                o = jnp.where(alive, o, jnp.zeros_like(o)).astype(BF)
                ctx[pl.ds(row, TT), heads[h]] = o.T
                lo = h * HD
                while lo < (h + 1) * HD:
                    piece, at = lo // HALF, lo % HALF
                    hi = min((h + 1) * HD, (piece + 1) * HALF)
                    ctxt[piece % 2, pl.ds((piece // 2) * HALF + at, hi - lo), pl.ds(row, TT)] = o[lo - h * HD:hi - h * HD]
                    lo = hi
            return carry

        lax.fori_loop(0, OWN, tile, 0)

    def grad_piece(half, col, width, store):
        for j in range(0, width, 256):
            wide = min(256, width - j)
            r = jnp.dot(ctxt[half], cot[:, col + j:col + j + wide], preferred_element_type=F32)
            for t in range(0, wide, 128):
                store((j + t) // 128, r[:, t:t + 128].reshape(NY, HALF, 128))

    def grad_sib(u):
        if u == 0:
            load_cot.wait()
        if u < 3:
            def store(t, r):
                gs[u, t] = r.astype(BF)
            grad_piece(sib, u * 512, 512, store)
            send(("g", u), gs.at[u], gr.at[u], sibling)
        else:
            def store(t, r):
                gs3[...] = r.astype(BF)
            grad_piece(sib, 1536, 128, store)
            send(("g", u), gs3, gr3, sibling)

    def grad_own(u):
        if u < 3:
            def store(t, r):
                gown[u, t] = r
            grad_piece(c, u * 512, 512, store)
        else:
            def store(t, r):
                gown3[...] = r
            grad_piece(c, 1536, 128, store)

    def two(body):
        lax.fori_loop(0, 2, lambda i, carry: (body(i), carry)[1], 0)

    def pair(u, t, yy):
        return gown[u, t, yy] + gr[u, t, yy].astype(F32)

    def x1(u):
        arrived(("g", u), gr.at[u])
        o2, o1, o3 = at_x(2), at_x(1), at_x(3)

        def body(i):
            xs2[u, i] = pair(u, o2, i).astype(BF)
            xs2[u, i + 2] = pair(u, o2, i + 2).astype(BF)

        two(body)
        send(("xa", u), xs2.at[u, pl.ds(0, 2)], ra.at[u, 0], right_x)
        send(("xa", u), xs2.at[u, pl.ds(2, 2)], ra.at[u, 1], left_x)

        def body(i):
            xs1[u, i] = pair(u, o1, i + 2).astype(BF)
            xs3[u, i] = pair(u, o3, i).astype(BF)

        two(body)
        send(("xb", u), xs1.at[u], rb.at[u, 0], right_x)
        send(("xb", u), xs3.at[u], rb.at[u, 1], left_x)

    def x2(u):
        arrived(("xa", u), ra.at[u])
        o1, o3 = at_x(1), at_x(3)

        def body(i):
            xt[u, 0, i] = (pair(u, o1, i) + ra[u, 0, i].astype(F32)).astype(BF)
            xt[u, 1, i] = (pair(u, o3, i + 2) + ra[u, 1, i].astype(F32)).astype(BF)

        two(body)
        send(("xb", u), xt.at[u, 0], rb.at[u, 2], right_x)
        send(("xb", u), xt.at[u, 1], rb.at[u, 3], left_x)

    def x3(u):
        if u < 3:
            arrived(("xb", u), rb.at[u])

            def body(i):
                a = pair(u, x, i) + rb[u, 2, i].astype(F32) + rb[u, 1, i].astype(F32)
                b = pair(u, x, i + 2) + rb[u, 0, i].astype(F32) + rb[u, 3, i].astype(F32)
                gown[u, x, i] = a
                gown[u, x, i + 2] = b
                ys[u, i] = a.astype(BF)
                ys[u, i + 2] = b.astype(BF)
        else:
            arrived(("g", u), gr3)

            def body(i):
                for j in (i, i + 2):
                    a = gown3[j] + gr3[j].astype(F32)
                    gown3[j] = a
                    ys[u, j] = a.astype(BF)

        two(body)
        for d in (1, 2, 3):
            send(("y", u), ys.at[u, at_y(d)], yr.at[u, d - 1], dev(at_y(d), z, c, x))

    def y2(u):
        arrived(("y", u), yr.at[u])
        total = gown[u, x, y] if u < 3 else gown3[y]
        for d in range(3):
            total = total + yr[u, d].astype(F32)
        zo[u] = total
        zs[u] = total.astype(BF)
        for i in range(4):
            zt = 4 * c + i
            slot = jnp.maximum(lax.rem(z - zt + NZ, NZ) - 1, 0)
            one = remote(("z", u), zs.at[u, pl.ds(48 * i, 64)], zr.at[u, slot], dev(y, zt, c, x))

            @pl.when(zt != z)
            def _():
                one.start()

    def z2(u):
        sem(("f", u))

        @pl.when(owner)
        def _():
            remote(("z", u), zr.at[u], zr.at[u], sibling).wait_recv()
            total = zo[u, pl.ds(pl.multiple_of(48 * zl, 16), 64), :]
            for d in range(7):
                total = total + zr[u, d].astype(F32)
            fr[u, x] = total.astype(BF)
            for d in range(4):
                for cc in (c, sib):
                    if d == 0 and cc is c:
                        continue
                    send(("f", u), fr.at[u, x], fr.at[u, x], dev(y, z, cc, at_x(d)))

    def f2(u):
        @pl.when(owner)
        def _():
            remote(("f", u), fr.at[u, pl.ds(0, 3)], fr.at[u, pl.ds(0, 3)], sibling).wait_recv()

        @pl.when(jnp.logical_not(owner))
        def _():
            remote(("f", u), fr.at[u], fr.at[u], sibling).wait_recv()

        if u < 3:
            for t in range(4):
                col = (4 * u + t) * 128
                grad_ref[:, col:col + 128] = fr[u, t].astype(F32) * SCALE
        else:
            total = fr[u, 0].astype(F32)
            for t in (1, 2, 3):
                total = total + fr[u, t].astype(F32)
            grad_ref[:, 1536:F] = total * SCALE

    def drain():
        sizes["as"], sizes["bs"] = wa.at[c], wb.at[c]
        for group, size in sizes.items():
            remote(group, size, size, sibling).wait_send()
        for u in range(4):
            @pl.when(owner)
            def _():
                three = zr.at[u, pl.ds(0, 3)]
                remote(("z", u), three, three, sibling).wait_send()
                remote(("f", u), zr.at[u], zr.at[u], sibling).wait_send()

            @pl.when(jnp.logical_not(owner))
            def _():
                four = zr.at[u, pl.ds(0, 4)]
                remote(("z", u), four, four, sibling).wait_send()

    def place(src, dst, width, lo, hi):
        r = lax.broadcasted_iota(jnp.int32, (HALF, 8 * PAD), 0)
        s = lax.broadcasted_iota(jnp.int32, (HALF, 8 * PAD), 1)
        cc, zz, j = s // (4 * PAD), (s // PAD) % 4, s % PAD
        pick = jnp.where((j < BLK) & (r == (zz * 2 + cc) * BLK + j), 1.0, 0.0).astype(BF)

        def body(g, carry):
            yy, z0 = lax.div(g, 2), lax.rem(g, 2) * 4
            blocks = [src[cc, yy, lax.rem(z0 + i + 12 - z, NZ)] for cc in (0, 1) for i in range(4)]
            r = jnp.dot(pick, jnp.concatenate(blocks, axis=0), preferred_element_type=F32)
            dst[pl.ds(pl.multiple_of(g * HALF, 16), HALF), :] = r.astype(BF)
            return carry

        lax.fori_loop(lo, hi, body, 0)

    def place_a(i):
        if i == 0:
            arrived("as", wa.at[sib])
        place(wa, wra, WA, 4 * i, 4 * i + 4)

    def place_b(i):
        if i == 0:
            arrived("bs", wb.at[sib])
        place(wb, wrb, WB, 4 * i, 4 * i + 4)

    out_copies = []

    def project(i):
        w, col, at = (wra, 0, 256 * i) if i < 3 else (wrb, WA, 256 * (i - 3))
        wide = min(256, F - col - at)
        cols = slice(col + at, col + at + wide)
        r = jnp.dot(ctx[...], w[:, at:at + wide], preferred_element_type=F32)
        att[:, cols] = r.astype(BF)
        one = pltpu.make_async_copy(att.at[:, cols], out_hbm.at[:, cols], out_sem.at[i])
        one.start()
        out_copies.append(one)

    attend(0)
    barrier()
    a0()
    b0()
    attend(1)
    attend(2)
    grad_sib(0)
    a1()
    b1()
    grad_own(0)
    grad_sib(1)
    grad_own(1)
    grad_sib(2)
    x1(0)
    grad_own(2)
    x1(1)
    grad_sib(3)
    grad_own(3)
    x1(2)
    x3(3)
    a2()
    x2(0)
    b2()
    y2(3)
    x2(1)
    a3()
    b3()
    b5()
    z2(3)
    x2(2)
    a4()
    b4()
    x3(0)
    a5()
    x3(1)
    f2(3)
    place_a(0)
    b6()
    place_a(1)
    x3(2)
    y2(0)
    project(0)
    project(1)
    y2(1)
    project(2)
    b7()
    z2(0)
    place_b(0)
    z2(1)
    y2(2)
    place_b(1)
    project(3)
    project(4)
    project(5)
    project(6)
    z2(2)
    f2(0)
    f2(1)
    f2(2)
    drain()
    for one in out_copies:
        one.wait()
    assert len(ids) <= NSEM, len(ids)


def core(queries, keys, values, cotangent, counts, weight):
    any_spec = pl.BlockSpec(memory_space=pl.ANY)
    vmem = pl.BlockSpec(memory_space=pltpu.VMEM)
    tiles = (MICRO * OWN, TT, F)
    V = pltpu.VMEM
    scratch = [
        V(tiles, BF), V(tiles, BF), V(tiles, BF), V((ROWS, F), BF),
        V((ROWS, F), BF), V((2, NY * HALF, ROWS), BF), V((ROWS, F), BF),
        V((2, NY, NZ, PAD, WA), BF), V((2, NY, NZ, PAD, WB), BF), V((F, WA), BF), V((F, WB), BF),
        V((3, 4, NY, HALF, 128), BF), V((3, 4, NY, HALF, 128), F32), V((3, 4, NY, HALF, 128), BF),
        V((NY, HALF, 128), BF), V((NY, HALF, 128), F32), V((NY, HALF, 128), BF),
    ]
    scratch += [
        V((3, 4, HALF, 128), BF), V((3, 2, HALF, 128), BF), V((3, 2, HALF, 128), BF),
        V((3, 2, 2, HALF, 128), BF), V((3, 2, 2, HALF, 128), BF), V((3, 4, 2, HALF, 128), BF),
        V((4, NY, HALF, 128), BF), V((4, 3, HALF, 128), BF),
        V((4, HALF, 128), BF), V((4, HALF, 128), F32), V((4, 7, 64, 128), BF), V((4, 4, 64, 128), BF),
        pltpu.SemaphoreType.DMA((10,)), pltpu.SemaphoreType.DMA((7,)),
        pltpu.SemaphoreType.DMA((NSEM,)), pltpu.SemaphoreType.DMA((NSEM,)),
    ]
    return pl.pallas_call(
        kernel,
        out_shape=[jax.ShapeDtypeStruct((ROWS, F), BF), jax.ShapeDtypeStruct((64, F), F32)],
        in_specs=[any_spec] * 4 + [pl.BlockSpec(memory_space=pltpu.SMEM), vmem],
        out_specs=[any_spec, vmem],
        scratch_shapes=scratch,
        compiler_params=pltpu.CompilerParams(
            collective_id=0, has_side_effects=True, vmem_limit_bytes=60 * 1024 * 1024),
        cost_estimate=pl.CostEstimate(flops=9_200_000_000, bytes_accessed=20_000_000, transcendentals=1_300_000),
    )(queries, keys, values, cotangent, counts, weight)


def local(queries, keys, values, cotangent, counts, out_weight):
    tiles = (MICRO * OWN, TT, F)
    attended, rows = core(
        queries.reshape(tiles), keys.reshape(tiles), values.reshape(tiles),
        cotangent.reshape(ROWS, F), counts, out_weight)
    dp = lax.axis_index("dp")
    c, zl = lax.rem(dp, 2), lax.rem(lax.div(dp, 2), 4)
    grad = lax.dynamic_slice_in_dim(rows, 4 * zl + BLK * c, BLK, 0)
    return (attended.reshape(MICRO, OWN, TT, F), grad)


def solution(mesh):
    return jax.shard_map(
        local,
        mesh=mesh,
        in_specs=(
            P(None, ("dp", "bal"), None, None),
            P(None, ("dp", "bal"), None, None),
            P(None, ("dp", "bal"), None, None),
            P(None, ("dp", "bal"), None, None),
            P(None, "dp", None),
            P("dp", None),
        ),
        out_specs=(P(None, ("dp", "bal"), None, None), P("dp", None)),
        check_vma=False,
    )
```

time: 99 us -> 69.8 us (0.71)
  Pallas kernels: 93 us -> 63.9 us
    pallas_call x1, Pallas kernels: 93 us -> 63.9 us  [core(): pl.pallas_call(kernel, out_shape=[jax.ShapeDtypeStruct((ROWS, F), BF), ja...]
where the time goes in v2:
time: 69.8 us; the launch traced here: 69.6 us
  Pallas kernels  63.9 us (92%)
  local copies, waits for them, and re-layouts  5.05 us (7%)
    pallas_call x1, Pallas kernels, core(): pl.pallas_call(kernel, out_shape=[jax.ShapeDtypeStruct((ROWS, F), BF), ja...  63.9 us
    unnamed x1, local copies, waits for them, and re-layouts  3.38 us
    dynamic_slice x1, local copies, waits for them, and re-layouts, local(): grad = lax.dynamic_slice_in_dim(rows, 4 * zl + BLK * c, BLK, 0)  1.67 us

profile of v2, /device:TPU:1, one launch (start us, length us, event | category | flops | bytes accessed | tf_op | source)
XLA Modules:
  0.0 69.6 jit_solution(7722309951297563308)
XLA Ops:
  0.7 63.9 %shard_map.77 = (bf16[768,1664]{1,0:T(8,128)(2,1)}, f32[64,1664]{1,0:T(8,128)}) custom-call(bf16[6,128,1664]{2,1,0:T(8,128)(2,1)} %bitcast.6, bf16[6,128,1664]{2,1,0:T(8,128)(2,1)} %bitcast.7, bf16[6,128,1664]{2,1,0:T(8,128)(2,1)} %bitcast.8, bf16[768,1664]{1,0:T(8,128)(2,1)} %bitcast.9, s32[3,1,4]{2,1,0:T(1,128)} %counts.1, bf16[26,1664]{1,0:T(8,128)(2,1)} %w_ref.1), custom_call_target="tpu_custom_call" | custom-call | flops 9200000000 | bytes 20000000 | tf_op jit(solution)/shard_map/pallas_call | solution.py:524
  64.5 1.7 %constant_dynamic-slice_fusion = f32[26,1664]{1,0:T(8,128)} fusion(f32[64,1664]{1,0:T(8,128)} %get-tuple-element.5, s32[]{:T(128)S(6)} %select_n.3), kind=kLoop, calls=%fused_computation | loop fusion | bytes 346116 | tf_op jit(solution)/shard_map/dynamic_slice | solution.py:543
  66.2 3.4 %copy.9 = bf16[3,2,128,1664]{3,2,1,0:T(8,128)(2,1)} copy(bf16[3,2,128,1664]{3,2,1,0:T(8,128)(2,1)} %bitcast.5) | data formatting | bytes 5111808

commit v3 on v2

--- a/solution.py
+++ b/solution.py
@@ -25,11 +25,11 @@
 MESH = pl.DeviceIdType.MESH
 F32 = jnp.float32
 BF = jnp.bfloat16
-NSEM = 48
-
-
-def kernel(q_hbm, k_hbm, v_hbm, cot_hbm, counts, w_ref, out_hbm, grad_ref,
-           q, k, v, cot, ctx, ctxt, att, wa, wb, wra, wrb,
+NSEM = 52
+
+
+def kernel(q_hbm, k_hbm, v_hbm, cot_hbm, counts_hbm, w_hbm, out_hbm, grad_ref,
+           counts, w_ref, q, k, v, cot, ctx, ctxt, att, wa, wb, wra, wrb,
            gs, gown, gr, gs3, gown3, gr3,
            xs2, xs1, xs3, xt, ra, rb,
            ys, yr, zs, zo, zr, fr,
@@ -80,6 +80,10 @@
         sizes[group] = size
         remote(group, size, size, sibling).wait_recv()
 
+    load_w = pltpu.make_async_copy(w_hbm, w_ref, in_sem.at[10])
+    load_counts = pltpu.make_async_copy(counts_hbm, counts, in_sem.at[11])
+    load_w.start()
+    load_counts.start()
     loads = {}
     n_in = 0
     for m in range(MICRO):
@@ -99,55 +103,57 @@
     for one in partners:
         pl.semaphore_signal(barrier_sem, inc=1, device_id=one, device_id_type=MESH)
 
-    wa[c, y, 4, pl.ds(16, 16), :] = jnp.zeros((16, WA), BF)
+    load_w.wait()
+    load_counts.wait()
+    for p in range(3):
+        wa[p, c, y, 4, pl.ds(16, 16), :] = jnp.zeros((16, 256), BF)
+        wa[p, c, y, 4, pl.ds(0, BLK), :] = w_ref[:, 256 * p:256 * p + 256]
     wb[c, y, 4, pl.ds(16, 16), :] = jnp.zeros((16, WB), BF)
-    wa[c, y, 4, pl.ds(0, BLK), :] = w_ref[:, 0:WA]
     wb[c, y, 4, pl.ds(0, BLK), :] = w_ref[:, WA:F]
 
     def barrier():
         pl.semaphore_wait(barrier_sem, len(partners))
 
-    def line(r):
-        return wa.at[c, :, r]
-
     def a0():
-        mine = wa.at[c, y, 4]
-        for d in (1, 2, 3):
-            send("ay", mine, mine, dev(at_y(d), z, c, x))
-
-    def a_ring(step):
+        for p in range(3):
+            mine = wa.at[p, c, y, 4]
+            for d in (1, 2, 3):
+                send(("ay", p), mine, mine, dev(at_y(d), z, c, x))
+
+    def a_ring(p, step):
         if step < 4:
-            send(("az", step), line(5 - step), line(4 - step), up_z)
-            send(("az", step), line(3 + step), line(4 + step), down_z)
+            send(("az", p, step), wa.at[p, c, :, 5 - step], wa.at[p, c, :, 4 - step], up_z)
+            send(("az", p, step), wa.at[p, c, :, 3 + step], wa.at[p, c, :, 4 + step], down_z)
         else:
-            send(("az", step), wa.at[c, :, 1, pl.ds(0, 16), :], wa.at[c, :, 0, pl.ds(0, 16), :], up_z)
-            send(("az", step), wa.at[c, :, 7, pl.ds(16, 16), :], wa.at[c, :, 0, pl.ds(16, 16), :], down_z)
-
-    def a_sib(lo, n):
-        ref = wa.at[c, :, pl.ds(lo, n)]
-        send("as", ref, ref, sibling)
-
-    def a1():
-        arrived("ay", wa.at[c, pl.ds(0, 3), 4])
-        a_ring(1)
-
-    def a2():
-        arrived(("az", 1), wa.at[c, :, pl.ds(0, 2)])
-        a_ring(2)
-
-    def a3():
-        arrived(("az", 2), wa.at[c, :, pl.ds(0, 2)])
-        a_ring(3)
-        a_sib(2, 5)
-
-    def a4():
-        arrived(("az", 3), wa.at[c, :, pl.ds(0, 2)])
-        a_ring(4)
-
-    def a5():
-        arrived(("az", 4), line(0))
-        a_sib(0, 2)
-        a_sib(7, 1)
+            lo, hi = pl.ds(0, 16), pl.ds(16, 16)
+            send(("az", p, step), wa.at[p, c, :, 1, lo, :], wa.at[p, c, :, 0, lo, :], up_z)
+            send(("az", p, step), wa.at[p, c, :, 7, hi, :], wa.at[p, c, :, 0, hi, :], down_z)
+
+    def a_sib(p, lo, n):
+        ref = wa.at[p, c, :, pl.ds(lo, n)]
+        send(("as", p), ref, ref, sibling)
+
+    def a1(p):
+        arrived(("ay", p), wa.at[p, c, pl.ds(0, 3), 4])
+        a_ring(p, 1)
+
+    def a2(p):
+        arrived(("az", p, 1), wa.at[p, c, :, pl.ds(0, 2)])
+        a_ring(p, 2)
+
+    def a3(p):
+        arrived(("az", p, 2), wa.at[p, c, :, pl.ds(0, 2)])
+        a_ring(p, 3)
+        a_sib(p, 2, 5)
+
+    def a4(p):
+        arrived(("az", p, 3), wa.at[p, c, :, pl.ds(0, 2)])
+        a_ring(p, 4)
+
+    def a5(p):
+        arrived(("az", p, 4), wa.at[p, c, :, 0])
+        a_sib(p, 0, 2)
+        a_sib(p, 7, 1)
 
     def block(r):
         return wb.at[c, y, r]
@@ -276,9 +282,9 @@
     def pair(u, t, yy):
         return gown[u, t, yy] + gr[u, t, yy].astype(F32)
 
-    def x1(u):
+    def x1a(u):
         arrived(("g", u), gr.at[u])
-        o2, o1, o3 = at_x(2), at_x(1), at_x(3)
+        o2 = at_x(2)
 
         def body(i):
             xs2[u, i] = pair(u, o2, i).astype(BF)
@@ -287,6 +293,9 @@
         two(body)
         send(("xa", u), xs2.at[u, pl.ds(0, 2)], ra.at[u, 0], right_x)
         send(("xa", u), xs2.at[u, pl.ds(2, 2)], ra.at[u, 1], left_x)
+
+    def x1b(u):
+        o1, o3 = at_x(1), at_x(3)
 
         def body(i):
             xs1[u, i] = pair(u, o1, i + 2).astype(BF)
@@ -384,7 +393,9 @@
             grad_ref[:, 1536:F] = total * SCALE
 
     def drain():
-        sizes["as"], sizes["bs"] = wa.at[c], wb.at[c]
+        sizes["bs"] = wb.at[c]
+        for p in range(3):
+            sizes["as", p] = wa.at[p, c]
         for group, size in sizes.items():
             remote(group, size, size, sibling).wait_send()
         for u in range(4):
@@ -414,10 +425,9 @@
 
         lax.fori_loop(lo, hi, body, 0)
 
-    def place_a(i):
-        if i == 0:
-            arrived("as", wa.at[sib])
-        place(wa, wra, WA, 4 * i, 4 * i + 4)
+    def place_a(p):
+        arrived(("as", p), wa.at[p, sib])
+        place(wa.at[p], wra.at[p], 256, 0, 8)
 
     def place_b(i):
         if i == 0:
@@ -427,7 +437,7 @@
     out_copies = []
 
     def project(i):
-        w, col, at = (wra, 0, 256 * i) if i < 3 else (wrb, WA, 256 * (i - 3))
+        w, col, at = (wra.at[i], 256 * i, 0) if i < 3 else (wrb, WA, 256 * (i - 3))
         wide = min(256, F - col - at)
         cols = slice(col + at, col + at + wide)
         r = jnp.dot(ctx[...], w[:, at:at + wide], preferred_element_type=F32)
@@ -438,62 +448,76 @@
 
     attend(0)
     barrier()
+    b0()
     a0()
-    b0()
     attend(1)
     attend(2)
+    b1()
     grad_sib(0)
-    a1()
-    b1()
     grad_own(0)
     grad_sib(1)
+    a1(0)
+    a1(1)
+    a1(2)
     grad_own(1)
+    x1a(0)
+    x1b(0)
+    b2()
     grad_sib(2)
-    x1(0)
+    x1a(1)
+    x1b(1)
     grad_own(2)
-    x1(1)
+    a2(0)
     grad_sib(3)
     grad_own(3)
-    x1(2)
+    x1a(2)
+    x1b(2)
+    a2(1)
+    x2(0)
     x3(3)
-    a2()
-    x2(0)
-    b2()
-    y2(3)
-    x2(1)
-    a3()
+    a2(2)
     b3()
     b5()
+    a3(0)
+    x2(1)
+    a3(1)
+    y2(3)
+    a3(2)
+    b4()
+    a4(0)
+    x2(2)
+    a4(1)
     z2(3)
-    x2(2)
-    a4()
-    b4()
+    b6()
+    a4(2)
+    a5(0)
     x3(0)
-    a5()
+    a5(1)
+    place_a(0)
+    a5(2)
+    place_a(1)
     x3(1)
-    f2(3)
-    place_a(0)
-    b6()
-    place_a(1)
+    b7()
+    place_a(2)
+    project(0)
+    y2(0)
     x3(2)
-    y2(0)
-    project(0)
     project(1)
+    project(2)
     y2(1)
-    project(2)
-    b7()
+    place_b(0)
     z2(0)
-    place_b(0)
+    place_b(1)
+    y2(2)
+    project(3)
     z2(1)
-    y2(2)
-    place_b(1)
-    project(3)
     project(4)
     project(5)
     project(6)
+    f2(0)
     z2(2)
-    f2(0)
     f2(1)
+    f2(3)
     f2(2)
     drain()
     for one in out_copies:
@@ -502,14 +526,16 @@
 
 
 def core(queries, keys, values, cotangent, counts, weight):
+    hbm = pl.BlockSpec(memory_space=pltpu.HBM)
     any_spec = pl.BlockSpec(memory_space=pl.ANY)
     vmem = pl.BlockSpec(memory_space=pltpu.VMEM)
     tiles = (MICRO * OWN, TT, F)
     V = pltpu.VMEM
     scratch = [
+        pltpu.SMEM((MICRO, 1, NX), jnp.int32), V((BLK, F), BF),
         V(tiles, BF), V(tiles, BF), V(tiles, BF), V((ROWS, F), BF),
         V((ROWS, F), BF), V((2, NY * HALF, ROWS), BF), V((ROWS, F), BF),
-        V((2, NY, NZ, PAD, WA), BF), V((2, NY, NZ, PAD, WB), BF), V((F, WA), BF), V((F, WB), BF),
+        V((3, 2, NY, NZ, PAD, 256), BF), V((2, NY, NZ, PAD, WB), BF), V((3, F, 256), BF), V((F, WB), BF),
         V((3, 4, NY, HALF, 128), BF), V((3, 4, NY, HALF, 128), F32), V((3, 4, NY, HALF, 128), BF),
         V((NY, HALF, 128), BF), V((NY, HALF, 128), F32), V((NY, HALF, 128), BF),
     ]
@@ -518,17 +544,17 @@
         V((3, 2, 2, HALF, 128), BF), V((3, 2, 2, HALF, 128), BF), V((3, 4, 2, HALF, 128), BF),
         V((4, NY, HALF, 128), BF), V((4, 3, HALF, 128), BF),
         V((4, HALF, 128), BF), V((4, HALF, 128), F32), V((4, 7, 64, 128), BF), V((4, 4, 64, 128), BF),
-        pltpu.SemaphoreType.DMA((10,)), pltpu.SemaphoreType.DMA((7,)),
+        pltpu.SemaphoreType.DMA((12,)), pltpu.SemaphoreType.DMA((7,)),
         pltpu.SemaphoreType.DMA((NSEM,)), pltpu.SemaphoreType.DMA((NSEM,)),
     ]
     return pl.pallas_call(
         kernel,
         out_shape=[jax.ShapeDtypeStruct((ROWS, F), BF), jax.ShapeDtypeStruct((64, F), F32)],
-        in_specs=[any_spec] * 4 + [pl.BlockSpec(memory_space=pltpu.SMEM), vmem],
+        in_specs=[hbm] * 6,
         out_specs=[any_spec, vmem],
         scratch_shapes=scratch,
         compiler_params=pltpu.CompilerParams(
-            collective_id=0, has_side_effects=True, vmem_limit_bytes=60 * 1024 * 1024),
+            collective_id=0, has_side_effects=True, vmem_limit_bytes=50 * 1024 * 1024),
         cost_estimate=pl.CostEstimate(flops=9_200_000_000, bytes_accessed=20_000_000, transcendentals=1_300_000),
     )(queries, keys, values, cotangent, counts, weight)
 

time: 69.8 us -> 65.7 us (0.941)
  Pallas kernels: 63.9 us -> 61.2 us
  local copies, waits for them, and re-layouts: 5.05 us -> 3.75 us
    pallas_call x1, Pallas kernels: 63.9 us -> 61.2 us  [core(): pl.pallas_call(kernel, out_shape=[jax.ShapeDtypeStruct((ROWS, F), BF), ja...]
    dynamic_slice x1, local copies, waits for them, and re-layouts: 1.67 us -> 0.71 us  [local(): grad = lax.dynamic_slice_in_dim(rows, 4 * zl + BLK * c, BLK, 0)]
    unnamed x1 -> x5, local copies, waits for them, and re-layouts: 3.38 us -> 3.04 us
where the time goes in v3:
time: 65.7 us; the launch traced here: 65.6 us
  Pallas kernels  61.2 us (93%)
  local copies, waits for them, and re-layouts  3.75 us (6%)
  between operations  0.67 us (1%)
    pallas_call x1, Pallas kernels, core(): pl.pallas_call(kernel, out_shape=[jax.ShapeDtypeStruct((ROWS, F), BF), ja...  61.2 us
    unnamed x5, local copies, waits for them, and re-layouts  3.04 us

profile of v3, /device:TPU:1, one launch (start us, length us, event | category | flops | bytes accessed | tf_op | source)
XLA Modules:
  0.0 65.6 jit_solution(6423694602581949794)
XLA Ops:
  0.7 0.0 copy-start
  0.7 0.9 %copy-done = bf16[26,1664]{1,0:T(8,128)(2,1)S(1)} copy-done((bf16[26,1664]{1,0:T(8,128)(2,1)S(1)}, bf16[26,1664]{1,0:T(8,128)(2,1)}, u32[]{:S(2)}) %copy-start) | copy-done | bytes 86552
  1.5 0.0 copy-start.1
  1.6 0.7 %copy-done.1 = s32[3,1,4]{2,1,0:T(1,128)S(1)} copy-done((s32[3,1,4]{2,1,0:T(1,128)S(1)}, s32[3,1,4]{2,1,0:T(1,128)}, u32[]{:S(2)}) %copy-start.1) | copy-done | bytes 72
  2.2 61.2 %shard_map.77 = (bf16[768,1664]{1,0:T(8,128)(2,1)S(1)}, f32[64,1664]{1,0:T(8,128)S(1)}) custom-call(bf16[6,128,1664]{2,1,0:T(8,128)(2,1)} %bitcast.6, bf16[6,128,1664]{2,1,0:T(8,128)(2,1)} %bitcast.7, bf16[6,128,1664]{2,1,0:T(8,128)(2,1)} %bitcast.8, bf16[768,1664]{1,0:T(8,128)(2,1)} %bitcast.9, s32[3,1,4]{2,1,0:T(1,128)S(1)} %copy-done.1, ...), custom_call_target="tpu_custom_call" | custom-call | flops 9200000000 | bytes 20000000 | tf_op jit(solution)/shard_map/pallas_call | solution.py:550
  63.4 0.7 %constant_dynamic-slice_fusion = f32[26,1664]{1,0:T(8,128)} fusion(f32[64,1664]{1,0:T(8,128)S(1)} %get-tuple-element.5, s32[]{:T(128)S(6)} %select_n.3), kind=kLoop, calls=%fused_computation | loop fusion | bytes 346116 | tf_op jit(solution)/shard_map/dynamic_slice | solution.py:569
  64.1 1.5 %copy.9 = bf16[3,2,128,1664]{3,2,1,0:T(8,128)(2,1)} copy(bf16[3,2,128,1664]{3,2,1,0:T(8,128)(2,1)S(1)} %bitcast.5) | data formatting | bytes 5111808
Async XLA Ops:
  0.7 0.9 %copy-start = (bf16[26,1664]{1,0:T(8,128)(2,1)S(1)}, bf16[26,1664]{1,0:T(8,128)(2,1)}, u32[]{:S(2)}) copy-start(bf16[26,1664]{1,0:T(8,128)(2,1)} %w_hbm.1) | copy-start | bytes 259588
  1.5 0.7 %copy-start.1 = (s32[3,1,4]{2,1,0:T(1,128)S(1)}, s32[3,1,4]{2,1,0:T(1,128)}, u32[]{:S(2)}) copy-start(s32[3,1,4]{2,1,0:T(1,128)} %counts_hbm.1) | copy-start | bytes 148

commit v4 on v3

--- a/solution.py
+++ b/solution.py
@@ -392,13 +392,11 @@
                 total = total + fr[u, t].astype(F32)
             grad_ref[:, 1536:F] = total * SCALE
 
-    def drain():
-        sizes["bs"] = wb.at[c]
-        for p in range(3):
-            sizes["as", p] = wa.at[p, c]
+    def drain(units):
         for group, size in sizes.items():
             remote(group, size, size, sibling).wait_send()
-        for u in range(4):
+        sizes.clear()
+        for u in units:
             @pl.when(owner)
             def _():
                 three = zr.at[u, pl.ds(0, 3)]
@@ -518,10 +516,14 @@
     z2(2)
     f2(1)
     f2(3)
-    f2(2)
-    drain()
+    sizes["bs"] = wb.at[c]
+    for p in range(3):
+        sizes["as", p] = wa.at[p, c]
+    drain((0, 1, 3))
     for one in out_copies:
         one.wait()
+    f2(2)
+    drain((2,))
     assert len(ids) <= NSEM, len(ids)
 
 

time: 65.7 us -> 65.6 us (level)
  no operation moved by 1% of the time
where the time goes in v4:
time: 65.6 us; the launch traced here: 65.5 us
  Pallas kernels  61.1 us (93%)
  local copies, waits for them, and re-layouts  3.75 us (6%)
  between operations  0.67 us (1%)
    pallas_call x1, Pallas kernels, core(): pl.pallas_call(kernel, out_shape=[jax.ShapeDtypeStruct((ROWS, F), BF), ja...  61.1 us
    unnamed x5, local copies, waits for them, and re-layouts  3.04 us

profile of v4, /device:TPU:1, one launch (start us, length us, event | category | flops | bytes accessed | tf_op | source)
XLA Modules:
  0.0 65.5 jit_solution(532429806076931920)
XLA Ops:
  0.7 0.0 copy-start
  0.7 0.9 %copy-done = bf16[26,1664]{1,0:T(8,128)(2,1)S(1)} copy-done((bf16[26,1664]{1,0:T(8,128)(2,1)S(1)}, bf16[26,1664]{1,0:T(8,128)(2,1)}, u32[]{:S(2)}) %copy-start) | copy-done | bytes 86552
  1.5 0.0 copy-start.1
  1.6 0.7 %copy-done.1 = s32[3,1,4]{2,1,0:T(1,128)S(1)} copy-done((s32[3,1,4]{2,1,0:T(1,128)S(1)}, s32[3,1,4]{2,1,0:T(1,128)}, u32[]{:S(2)}) %copy-start.1) | copy-done | bytes 72
  2.2 61.1 %shard_map.77 = (bf16[768,1664]{1,0:T(8,128)(2,1)S(1)}, f32[64,1664]{1,0:T(8,128)S(1)}) custom-call(bf16[6,128,1664]{2,1,0:T(8,128)(2,1)} %bitcast.6, bf16[6,128,1664]{2,1,0:T(8,128)(2,1)} %bitcast.7, bf16[6,128,1664]{2,1,0:T(8,128)(2,1)} %bitcast.8, bf16[768,1664]{1,0:T(8,128)(2,1)} %bitcast.9, s32[3,1,4]{2,1,0:T(1,128)S(1)} %copy-done.1, ...), custom_call_target="tpu_custom_call" | custom-call | flops 9200000000 | bytes 20000000 | tf_op jit(solution)/shard_map/pallas_call | solution.py:552
  63.3 0.7 %constant_dynamic-slice_fusion = f32[26,1664]{1,0:T(8,128)} fusion(f32[64,1664]{1,0:T(8,128)S(1)} %get-tuple-element.5, s32[]{:T(128)S(6)} %select_n.3), kind=kLoop, calls=%fused_computation | loop fusion | bytes 346116 | tf_op jit(solution)/shard_map/dynamic_slice | solution.py:571
  64.0 1.5 %copy.9 = bf16[3,2,128,1664]{3,2,1,0:T(8,128)(2,1)} copy(bf16[3,2,128,1664]{3,2,1,0:T(8,128)(2,1)S(1)} %bitcast.5) | data formatting | bytes 5111808
Async XLA Ops:
  0.7 0.9 %copy-start = (bf16[26,1664]{1,0:T(8,128)(2,1)S(1)}, bf16[26,1664]{1,0:T(8,128)(2,1)}, u32[]{:S(2)}) copy-start(bf16[26,1664]{1,0:T(8,128)(2,1)} %w_hbm.1) | copy-start | bytes 259588
  1.5 0.7 %copy-start.1 = (s32[3,1,4]{2,1,0:T(1,128)S(1)}, s32[3,1,4]{2,1,0:T(1,128)}, u32[]{:S(2)}) copy-start(s32[3,1,4]{2,1,0:T(1,128)} %counts_hbm.1) | copy-start | bytes 148

commit v5 on v4

--- a/solution.py
+++ b/solution.py
@@ -28,8 +28,8 @@
 NSEM = 52
 
 
-def kernel(q_hbm, k_hbm, v_hbm, cot_hbm, counts_hbm, w_hbm, out_hbm, grad_ref,
-           counts, w_ref, q, k, v, cot, ctx, ctxt, att, wa, wb, wra, wrb,
+def kernel(q_hbm, k_hbm, v_hbm, cot_hbm, counts, w_ref, out_hbm, grad_ref,
+           q, k, v, cot, ctx, ctxt, att, wa, wb, wra, wrb,
            gs, gown, gr, gs3, gown3, gr3,
            xs2, xs1, xs3, xt, ra, rb,
            ys, yr, zs, zo, zr, fr,
@@ -80,10 +80,6 @@
         sizes[group] = size
         remote(group, size, size, sibling).wait_recv()
 
-    load_w = pltpu.make_async_copy(w_hbm, w_ref, in_sem.at[10])
-    load_counts = pltpu.make_async_copy(counts_hbm, counts, in_sem.at[11])
-    load_w.start()
-    load_counts.start()
     loads = {}
     n_in = 0
     for m in range(MICRO):
@@ -103,8 +99,6 @@
     for one in partners:
         pl.semaphore_signal(barrier_sem, inc=1, device_id=one, device_id_type=MESH)
 
-    load_w.wait()
-    load_counts.wait()
     for p in range(3):
         wa[p, c, y, 4, pl.ds(16, 16), :] = jnp.zeros((16, 256), BF)
         wa[p, c, y, 4, pl.ds(0, BLK), :] = w_ref[:, 256 * p:256 * p + 256]
@@ -534,7 +528,6 @@
     tiles = (MICRO * OWN, TT, F)
     V = pltpu.VMEM
     scratch = [
-        pltpu.SMEM((MICRO, 1, NX), jnp.int32), V((BLK, F), BF),
         V(tiles, BF), V(tiles, BF), V(tiles, BF), V((ROWS, F), BF),
         V((ROWS, F), BF), V((2, NY * HALF, ROWS), BF), V((ROWS, F), BF),
         V((3, 2, NY, NZ, PAD, 256), BF), V((2, NY, NZ, PAD, WB), BF), V((3, F, 256), BF), V((F, WB), BF),
@@ -546,13 +539,13 @@
         V((3, 2, 2, HALF, 128), BF), V((3, 2, 2, HALF, 128), BF), V((3, 4, 2, HALF, 128), BF),
         V((4, NY, HALF, 128), BF), V((4, 3, HALF, 128), BF),
         V((4, HALF, 128), BF), V((4, HALF, 128), F32), V((4, 7, 64, 128), BF), V((4, 4, 64, 128), BF),
-        pltpu.SemaphoreType.DMA((12,)), pltpu.SemaphoreType.DMA((7,)),
+        pltpu.SemaphoreType.DMA((10,)), pltpu.SemaphoreType.DMA((7,)),
         pltpu.SemaphoreType.DMA((NSEM,)), pltpu.SemaphoreType.DMA((NSEM,)),
     ]
     return pl.pallas_call(
         kernel,
         out_shape=[jax.ShapeDtypeStruct((ROWS, F), BF), jax.ShapeDtypeStruct((64, F), F32)],
-        in_specs=[hbm] * 6,
+        in_specs=[hbm] * 4 + [pl.BlockSpec(memory_space=pltpu.SMEM), vmem],
         out_specs=[any_spec, vmem],
         scratch_shapes=scratch,
         compiler_params=pltpu.CompilerParams(

time: 65.6 us -> 66.2 us (level)
  no operation moved by 1% of the time
where the time goes in v5:
time: 66.2 us; the launch traced here: 66.1 us
  Pallas kernels  61.7 us (93%)
  local copies, waits for them, and re-layouts  3.75 us (6%)
  between operations  0.67 us (1%)
    pallas_call x1, Pallas kernels, core(): pl.pallas_call(kernel, out_shape=[jax.ShapeDtypeStruct((ROWS, F), BF), ja...  61.7 us
    unnamed x5, local copies, waits for them, and re-layouts  3.04 us

profile of v5, /device:TPU:1, one launch (start us, length us, event | category | flops | bytes accessed | tf_op | source)
XLA Modules:
  0.0 66.1 jit_solution(1726841728010236628)
XLA Ops:
  0.7 0.0 copy-start
  0.7 0.9 %copy-done = bf16[26,1664]{1,0:T(8,128)(2,1)S(1)} copy-done((bf16[26,1664]{1,0:T(8,128)(2,1)S(1)}, bf16[26,1664]{1,0:T(8,128)(2,1)}, u32[]{:S(2)}) %copy-start) | copy-done | bytes 86552
  1.5 0.0 copy-start.1
  1.6 0.7 %copy-done.1 = s32[3,1,4]{2,1,0:T(1,128)S(1)} copy-done((s32[3,1,4]{2,1,0:T(1,128)S(1)}, s32[3,1,4]{2,1,0:T(1,128)}, u32[]{:S(2)}) %copy-start.1) | copy-done | bytes 72
  2.2 61.7 %shard_map.77 = (bf16[768,1664]{1,0:T(8,128)(2,1)S(1)}, f32[64,1664]{1,0:T(8,128)S(1)}) custom-call(bf16[6,128,1664]{2,1,0:T(8,128)(2,1)} %bitcast.6, bf16[6,128,1664]{2,1,0:T(8,128)(2,1)} %bitcast.7, bf16[6,128,1664]{2,1,0:T(8,128)(2,1)} %bitcast.8, bf16[768,1664]{1,0:T(8,128)(2,1)} %bitcast.9, s32[3,1,4]{2,1,0:T(1,128)S(1)} %copy-done.1, ...), custom_call_target="tpu_custom_call" | custom-call | flops 9200000000 | bytes 20000000 | tf_op jit(solution)/shard_map/pallas_call | solution.py:545
  63.9 0.7 %constant_dynamic-slice_fusion = f32[26,1664]{1,0:T(8,128)} fusion(f32[64,1664]{1,0:T(8,128)S(1)} %get-tuple-element.5, s32[]{:T(128)S(6)} %select_n.3), kind=kLoop, calls=%fused_computation | loop fusion | bytes 346116 | tf_op jit(solution)/shard_map/dynamic_slice | solution.py:564
  64.6 1.5 %copy.9 = bf16[3,2,128,1664]{3,2,1,0:T(8,128)(2,1)} copy(bf16[3,2,128,1664]{3,2,1,0:T(8,128)(2,1)S(1)} %bitcast.5) | data formatting | bytes 5111808
Async XLA Ops:
  0.7 0.9 %copy-start = (bf16[26,1664]{1,0:T(8,128)(2,1)S(1)}, bf16[26,1664]{1,0:T(8,128)(2,1)}, u32[]{:S(2)}) copy-start(bf16[26,1664]{1,0:T(8,128)(2,1)} %w_ref.1) | copy-start | bytes 259588
  1.5 0.7 %copy-start.1 = (s32[3,1,4]{2,1,0:T(1,128)S(1)}, s32[3,1,4]{2,1,0:T(1,128)}, u32[]{:S(2)}) copy-start(s32[3,1,4]{2,1,0:T(1,128)} %counts.1) | copy-start | bytes 148
